TPU v7x, 256 devices: a whole 4x4x8 slice. The times are simulated.
256 devices in a mesh: orb: 8 (over x, z_hi), gx: 4 (over y), gy: 8 (over z_lo, core).
Axes of the slice: x: 4, y: 4, z: 8 (z_hi: 2, z_lo: 4; z = z_hi * 4 + z_lo), core: 2. Of those that a mesh axis runs over, the one named last changes fastest.
Arguments:
- orbitals: float32 [16, 48, 128, 512], P('orb', None, 'gy', 'gx'), may hold values from 1 to 2
- potential: float32 [48, 128, 512], P(None, 'gy', 'gx'), may hold values from 0 to 0.5
- cheb_coeffs: float32 [4], replicated, may hold values from 0.1 to 1, as said below
Outputs:
- density: float32 [48, 128, 512], P('orb', 'gy', 'gx')
Inputs may be any that keep to these rules, and one draw needn't show every extreme that they name: `cheb_coeffs`: 4 weights; the last one is 0.7 or more, the others 0.3 or less.
All inputs are finite; a program needn't handle non-finite values.
Results may differ from a plain program's by a relative error of at most 0.00002.
Values sent between devices are 32-bit elements; how exact they have to be, the bound alone decides.
A program may use at most 128 MiB of HBM per device.

v0:
```python
import jax
import jax.numpy as jnp
from jax import lax
from jax.sharding import PartitionSpec as P

CHEB = 3


STENCIL_COEFFS = (-205.0 / 72.0, 8.0 / 5.0, -1.0 / 5.0, 8.0 / 315.0, -1.0 / 560.0)
ENERGY_SHIFT = 5.875
ENERGY_SPREAD = 6.0


def padded_2(block, sides, width):
    for axis, dim in sides:
        count = lax.axis_size(axis)
        forward = [(i, i + 1) for i in range(count - 1)]
        forward.append((count - 1, 0))
        backward = [(target, source) for source, target in forward]
        low = lax.ppermute(
            lax.slice_in_dim(block, block.shape[dim] - width, None, axis=dim), axis, forward
        )
        high = lax.ppermute(lax.slice_in_dim(block, 0, width, axis=dim), axis, backward)
        block = jnp.concatenate([low, block, high], axis=dim)
    return block


def cut_along(shard, dim, length):
    shape = shard.shape
    parts = shard.reshape(*shape[:dim], length, shape[dim] // length, *shape[dim + 1 :])
    return jnp.moveaxis(parts, dim, 0)


def sum_at_owner(shard, axis, dim):
    length = lax.axis_size(axis)
    parts = lax.all_to_all(cut_along(shard, dim, length), axis, 0, 0, tiled=True)
    return jnp.sum(parts, axis=0)


def apply_hamiltonian(padded, potential_core):
    height = padded.shape[2] - 8
    breadth = padded.shape[3] - 8
    centre = padded[:, :, 4 : 4 + height, 4 : 4 + breadth]
    summed = 3.0 * STENCIL_COEFFS[0] * centre
    for offset in range(1, 5):
        summed = summed + STENCIL_COEFFS[offset] * (
            padded[:, :, 4 + offset : 4 + offset + height, 4 : 4 + breadth]
            + padded[:, :, 4 - offset : 4 - offset + height, 4 : 4 + breadth]
            + padded[:, :, 4 : 4 + height, 4 + offset : 4 + offset + breadth]
            + padded[:, :, 4 : 4 + height, 4 - offset : 4 - offset + breadth]
            + jnp.roll(centre, offset, 1)
            + jnp.roll(centre, -offset, 1)
        )
    return (-0.5 * summed + (potential_core[None] - ENERGY_SHIFT) * centre) / ENERGY_SPREAD


def local(orbitals, potential, cheb_coeffs):
    filtered = cheb_coeffs[0] * orbitals
    previous = orbitals
    current = orbitals
    for step in range(CHEB):
        padded = padded_2(current, (("gx", 3), ("gy", 2)), 4)
        applied = apply_hamiltonian(padded, potential)
        if step == 0:
            following = applied
        else:
            following = 2.0 * applied - previous
        filtered = filtered + cheb_coeffs[step + 1] * following
        previous, current = (current, following)
    squares = jnp.sum(filtered * filtered, axis=0)
    owned = sum_at_owner(squares, "orb", 0)
    return owned / (orbitals.shape[0] * lax.axis_size("orb"))


def solution(mesh):
    in_specs = (P("orb", None, "gy", "gx"), P(None, "gy", "gx"), P())
    out_specs = P("orb", "gy", "gx")
    return jax.shard_map(local, mesh=mesh, in_specs=in_specs, out_specs=out_specs, check_vma=False)
```

profile of v0, /device:TPU:1, one launch (start us, length us, event | category | flops | bytes accessed | tf_op | source)
XLA Modules:
  0.0 132.2 jit_solution(683466092841369988)
XLA Ops:
  0.0 1.7 %fusion.129 = (f32[2,48,16,4]{3,2,1,0:T(8,128)S(1)}, f32[2,48,16,4]{3,2,1,0:T(8,128)S(1)}) fusion(f32[2,48,16,128]{3,2,1,0:T(8,128)} %param.3), kind=kLoop, calls=%fused_computation.201 | loop fusion | bytes 98304 | tf_op jit(solution)/shard_map/slice | solution.py:23
  1.7 0.4 copy.134
  2.1 2.2 %collective-permute-start = (f32[2,48,16,4]{1,2,3,0:T(8,128)S(1)}, f32[2,48,16,4]{1,2,3,0:T(8,128)}, u32[]{:S(2)}, u32[]{:S(2)}) collective-permute-start(f32[2,48,16,4]{1,2,3,0:T(8,128)S(1)} %copy.134), channel_id=1, source_target_pairs={{0,8},{8,16},{16,24},{24,0},{1,9},{9,17},{17,25},{25,1},{2,10},{10... | collective-permute-start | bytes 73736 | tf_op jit(solution)/shard_map/ppermute | solution.py:20
  4.3 1.0 copy.135
  5.3 1.5 %collective-permute-start.1 = (f32[2,48,16,4]{1,2,3,0:T(8,128)}, f32[2,48,16,4]{1,2,3,0:T(8,128)}, u32[]{:S(2)}, u32[]{:S(2)}) collective-permute-start(f32[2,48,16,4]{1,2,3,0:T(8,128)} %copy.135), channel_id=1, source_target_pairs={{8,0},{16,8},{24,16},{0,24},{9,1},{17,9},{25,17},{1,25},{10,2},{18... | collective-permute-start | bytes 73736 | tf_op jit(solution)/shard_map/ppermute | solution.py:23
  7.0 1.2 fusion.124
  8.2 1.3 fusion.126
  9.5 1.3 fusion.128
  10.7 1.2 fusion.131
  12.0 0.7 fusion.127
  12.7 0.7 fusion.130
  13.3 0.7 fusion.125
  14.1 0.6 fusion.132
  14.8 0.9 copy.125
  16.4 1.2 copy.94
  17.6 1.2 copy.96
  18.7 0.4 pad_maximum_fusion.17
  19.1 3.0 %collective-permute-start.2 = (f32[2,48,4,136]{3,1,2,0:T(8,128)S(1)}, f32[2,48,4,136]{3,1,2,0:T(8,128)S(1)}, u32[]{:S(2)}, u32[]{:S(2)}) collective-permute-start(f32[2,48,4,136]{3,1,2,0:T(8,128)S(1)} %get-tuple-element.17), channel_id=1, source_target_pairs={{1,0},{2,1},{3,2},{4,3},{5,4},{6,5},{7,6},{0,7},{9,8},{10,9},{11,1... | collective-permute-start | bytes 626696 | tf_op jit(solution)/shard_map/ppermute | solution.py:23
  22.2 5.1 %collective-permute-done.2 = f32[2,48,4,136]{3,1,2,0:T(8,128)S(1)} collective-permute-done((f32[2,48,4,136]{3,1,2,0:T(8,128)S(1)}, f32[2,48,4,136]{3,1,2,0:T(8,128)S(1)}, u32[]{:S(2)}, u32[]{:S(2)}) %collective-permute-start.2) | collective-permute-done | bytes 208928 | tf_op jit(solution)/shard_map/ppermute | solution.py:23
  27.3 1.6 %collective-permute-done.3 = f32[2,48,4,136]{3,1,2,0:T(8,128)S(1)} collective-permute-done((f32[2,48,4,136]{3,1,2,0:T(8,128)S(1)}, f32[2,48,4,136]{3,1,2,0:T(8,128)S(1)}, u32[]{:S(2)}, u32[]{:S(2)}) %collective-permute-start.3) | collective-permute-done | bytes 208928 | tf_op jit(solution)/shard_map/ppermute | solution.py:20
  29.0 1.3 pad_maximum_fusion
  30.4 7.6 %broadcast_multiply_fusion = (f32[2,48,16,128]{3,1,2,0:T(8,128)S(1)}, f32[2,48,16,128]{3,1,2,0:T(8,128)}) fusion(f32[2,48,16,128]{3,1,2,0:T(8,128)S(1)} %copy.90, f32[48,16,128]{2,0,1:T(8,128)S(1)} %copy.117, f32[2,4,16,128]{3,1,2,0:T(4,128)S(1)} %copy-done.38, f32[2,44,16,128]{3,1,2,0:T(8,128)S(1)} %copy-done.20, f32[2,44,16,128]{3,1,2,0:T(8,128)S(1)} %copy-done.19, ...), kind=kLoop, calls=%fused_computation.173 | loop fusion | flops 9633792 | bytes 15384576 | tf_op jit(solution)/shard_map/div | solution.py:54
  38.0 0.3 fusion.122
  38.3 1.2 fusion.114
  39.6 1.3 fusion.116
  40.9 1.2 fusion.118
  42.1 1.2 fusion.120
  43.3 0.7 fusion.115
  44.0 0.7 fusion.117
  44.7 0.9 copy.119
  45.6 0.9 copy.120
  46.5 2.7 %collective-permute-start.5 = (f32[2,48,16,4]{1,2,3,0:T(8,128)}, f32[2,48,16,4]{1,2,3,0:T(8,128)}, u32[]{:S(2)}, u32[]{:S(2)}) collective-permute-start(f32[2,48,16,4]{1,2,3,0:T(8,128)} %copy.120), channel_id=1, source_target_pairs={{8,0},{16,8},{24,16},{0,24},{9,1},{17,9},{25,17},{1,25},{10,2},{18... | collective-permute-start | bytes 73736 | tf_op jit(solution)/shard_map/ppermute | solution.py:23
  49.2 0.6 fusion.119
  49.9 0.4 collective-permute-done.4
  50.3 1.2 copy.121
  51.5 1.2 copy.122
  52.7 0.4 pad_maximum_fusion.14
  53.1 7.2 %collective-permute-start.6 = (f32[2,48,4,136]{3,1,2,0:T(8,128)S(1)}, f32[2,48,4,136]{3,1,2,0:T(8,128)S(1)}, u32[]{:S(2)}, u32[]{:S(2)}) collective-permute-start(f32[2,48,4,136]{3,1,2,0:T(8,128)S(1)} %get-tuple-element.13), channel_id=1, source_target_pairs={{1,0},{2,1},{3,2},{4,3},{5,4},{6,5},{7,6},{0,7},{9,8},{10,9},{11,1... | collective-permute-start | bytes 626696 | tf_op jit(solution)/shard_map/ppermute | solution.py:23
  60.4 2.0 %collective-permute-done.6 = f32[2,48,4,136]{3,1,2,0:T(8,128)S(1)} collective-permute-done((f32[2,48,4,136]{3,1,2,0:T(8,128)S(1)}, f32[2,48,4,136]{3,1,2,0:T(8,128)S(1)}, u32[]{:S(2)}, u32[]{:S(2)}) %collective-permute-start.6) | collective-permute-done | bytes 208928 | tf_op jit(solution)/shard_map/ppermute | solution.py:23
  62.5 6.6 %collective-permute-done.7 = f32[2,48,4,136]{3,1,2,0:T(8,128)S(1)} collective-permute-done((f32[2,48,4,136]{3,1,2,0:T(8,128)S(1)}, f32[2,48,4,136]{3,1,2,0:T(8,128)S(1)}, u32[]{:S(2)}, u32[]{:S(2)}) %collective-permute-start.7) | collective-permute-done | bytes 208928 | tf_op jit(solution)/shard_map/ppermute | solution.py:20
  69.0 1.3 pad_maximum_fusion.1
  70.5 6.7 %fusion.42 = f32[2,48,16,128]{3,1,2,0:T(8,128)S(1)} fusion(f32[2,48,16,4]{3,1,2,0:T(8,128)S(1)} %copy.121, f32[2,48,16,128]{3,1,2,0:T(8,128)S(1)} %get-tuple-element.5, f32[2,48,16,4]{3,1,2,0:T(8,128)} %copy-done.2, f32[2,48,20,136]{3,1,2,0:T(8,128)S(1)} %get-tuple-element.12, f32[2,48,20,136]{3,1,2,0:T(8,128)S(1)} %get-tuple-element.11, ...), kind=kLoop, calls=%fused_computation.84 | loop fusion | flops 9830400 | bytes 16171008 | tf_op jit(solution)/shard_map/sub | solution.py:67
  77.2 0.3 fusion.111
  77.5 1.3 fusion.106
  78.8 1.3 fusion.108
  80.1 1.3 fusion.110
  81.3 1.3 fusion.113
  82.6 0.7 fusion.109
  83.3 0.7 fusion.112
  84.0 0.9 copy.127
  85.1 0.3 copy.128
  85.4 2.6 %collective-permute-start.9 = (f32[2,48,16,4]{1,2,3,0:T(8,128)S(1)}, f32[2,48,16,4]{1,2,3,0:T(8,128)}, u32[]{:S(2)}, u32[]{:S(2)}) collective-permute-start(f32[2,48,16,4]{1,2,3,0:T(8,128)S(1)} %copy.128), channel_id=1, source_target_pairs={{8,0},{16,8},{24,16},{0,24},{9,1},{17,9},{25,17},{1,25},{10,2},{18... | collective-permute-start | bytes 73736 | tf_op jit(solution)/shard_map/ppermute | solution.py:23
  88.0 0.6 fusion.107
  88.6 0.8 collective-permute-done.8
  89.4 0.3 copy.129
  89.8 1.2 copy.130
  91.0 0.4 pad_maximum_fusion.11
  91.4 4.0 %collective-permute-start.10 = (f32[2,48,4,136]{3,1,2,0:T(8,128)S(1)}, f32[2,48,4,136]{3,1,2,0:T(8,128)S(1)}, u32[]{:S(2)}, u32[]{:S(2)}) collective-permute-start(f32[2,48,4,136]{3,1,2,0:T(8,128)S(1)} %get-tuple-element.9), channel_id=1, source_target_pairs={{1,0},{2,1},{3,2},{4,3},{5,4},{6,5},{7,6},{0,7},{9,8},{10,9},{11,1... | collective-permute-start | bytes 626696 | tf_op jit(solution)/shard_map/ppermute | solution.py:23
  95.5 5.3 %collective-permute-done.10 = f32[2,48,4,136]{3,1,2,0:T(8,128)S(1)} collective-permute-done((f32[2,48,4,136]{3,1,2,0:T(8,128)S(1)}, f32[2,48,4,136]{3,1,2,0:T(8,128)S(1)}, u32[]{:S(2)}, u32[]{:S(2)}) %collective-permute-start.10) | collective-permute-done | bytes 208928 | tf_op jit(solution)/shard_map/ppermute | solution.py:23
  100.9 2.3 %collective-permute-done.11 = f32[2,48,4,136]{3,1,2,0:T(8,128)S(1)} collective-permute-done((f32[2,48,4,136]{3,1,2,0:T(8,128)S(1)}, f32[2,48,4,136]{3,1,2,0:T(8,128)S(1)}, u32[]{:S(2)}, u32[]{:S(2)}) %collective-permute-start.11) | collective-permute-done | bytes 208928 | tf_op jit(solution)/shard_map/ppermute | solution.py:20
  103.2 1.3 pad_maximum_fusion.2
  104.6 6.9 %fusion.103 = f32[48,16,128]{2,0,1:T(8,128)S(1)} fusion(f32[2,48,16,128]{3,1,2,0:T(8,128)S(1)} %fusion.42, f32[2,4,16,128]{3,1,2,0:T(4,128)S(1)} %copy-done.34, f32[2,44,16,128]{3,1,2,0:T(8,128)S(1)} %copy-done.16, f32[2,44,16,128]{3,1,2,0:T(8,128)S(1)} %copy-done.15, f32[2,4,16,128]{3,1,2,0:T(4,128)S(1)} %copy-done.33, f32[2,48,16,4]{3,1,2,0:T(8,128)S(1)} %copy.129, ...), kind=kLoop, calls=%fused_computation.163 | loop fusion | flops 11698176 | bytes 15777808 | tf_op jit(solution)/shard_map/reduce_sum | solution.py:70
  111.7 19.8 %all_to_all.5 = f32[8,6,16,128]{3,2,1,0:T(8,128)S(1)} all-to-all(f32[8,6,16,128]{3,2,1,0:T(8,128)S(1)} %bitcast.7), channel_id=1, replica_groups=mesh['orb'=8,'gx'=4,'gy'=8] {'orb'}, dimensions={0} | all-to-all | bytes 786432 | tf_op jit(solution)/shard_map/all_to_all | solution.py:36
  131.6 0.6 broadcast_multiply_fusion.2
  (117 shorter events, 1.1 us)
Async XLA Ops:
  0.0 6.7 %copy-start = (f32[2,48,16,128]{3,2,1,0:T(8,128)S(1)}, f32[2,48,16,128]{3,2,1,0:T(8,128)}, u32[]{:S(2)}) copy-start(f32[2,48,16,128]{3,2,1,0:T(8,128)} %param.3) | copy-start | bytes 2359300
  2.1 14.3 %collective-permute-start = (f32[2,48,16,4]{1,2,3,0:T(8,128)S(1)}, f32[2,48,16,4]{1,2,3,0:T(8,128)}, u32[]{:S(2)}, u32[]{:S(2)}) collective-permute-start(f32[2,48,16,4]{1,2,3,0:T(8,128)S(1)} %copy.134), channel_id=1, source_target_pairs={{0,8},{8,16},{16,24},{24,0},{1,9},{9,17},{17,25},{25,1},{2,10},{10... | collective-permute-start | bytes 73736 | tf_op jit(solution)/shard_map/ppermute | solution.py:20
  5.3 12.3 %collective-permute-start.1 = (f32[2,48,16,4]{1,2,3,0:T(8,128)}, f32[2,48,16,4]{1,2,3,0:T(8,128)}, u32[]{:S(2)}, u32[]{:S(2)}) collective-permute-start(f32[2,48,16,4]{1,2,3,0:T(8,128)} %copy.135), channel_id=1, source_target_pairs={{8,0},{16,8},{24,16},{0,24},{9,1},{17,9},{25,17},{1,25},{10,2},{18... | collective-permute-start | bytes 73736 | tf_op jit(solution)/shard_map/ppermute | solution.py:23
  10.7 3.3 %copy-start.30 = (f32[48,16,128]{2,1,0:T(8,128)S(1)}, f32[48,16,128]{2,1,0:T(8,128)}, u32[]{:S(2)}) copy-start(f32[48,16,128]{2,1,0:T(8,128)} %param.4) | copy-start | bytes 1179652
  10.7 3.3 %copy-start.49 = (f32[4]{0:T(128)S(1)}, f32[4]{0:T(128)}, u32[]{:S(2)}) copy-start(f32[4]{0:T(128)} %param.5) | copy-start | bytes 52
  18.7 11.5 %copy-start.1 = (f32[2,48,16,4]{3,1,2,0:T(8,128)}, f32[2,48,16,4]{3,1,2,0:T(8,128)S(1)}, u32[]{:S(2)}) copy-start(f32[2,48,16,4]{3,1,2,0:T(8,128)S(1)} %copy.96) | copy-start | bytes 73732
  19.1 8.2 %collective-permute-start.2 = (f32[2,48,4,136]{3,1,2,0:T(8,128)S(1)}, f32[2,48,4,136]{3,1,2,0:T(8,128)S(1)}, u32[]{:S(2)}, u32[]{:S(2)}) collective-permute-start(f32[2,48,4,136]{3,1,2,0:T(8,128)S(1)} %get-tuple-element.17), channel_id=1, source_target_pairs={{1,0},{2,1},{3,2},{4,3},{5,4},{6,5},{7,6},{0,7},{9,8},{10,9},{11,1... | collective-permute-start | bytes 626696 | tf_op jit(solution)/shard_map/ppermute | solution.py:23
  22.1 6.9 %collective-permute-start.3 = (f32[2,48,4,136]{3,1,2,0:T(8,128)S(1)}, f32[2,48,4,136]{3,1,2,0:T(8,128)S(1)}, u32[]{:S(2)}, u32[]{:S(2)}) collective-permute-start(f32[2,48,4,136]{3,1,2,0:T(8,128)S(1)} %get-tuple-element.18), channel_id=1, source_target_pairs={{0,1},{1,2},{2,3},{3,4},{4,5},{5,6},{6,7},{7,0},{8,9},{9,10},{10,1... | collective-permute-start | bytes 626696 | tf_op jit(solution)/shard_map/ppermute | solution.py:20
  22.1 8.2 %copy-start.9 = (f32[2,47,16,128]{3,1,2,0:T(8,128)S(1)}, f32[2,47,16,128]{3,1,2,0:T(8,128)}, u32[]{:S(2)}) copy-start(f32[2,47,16,128]{3,1,2,0:T(8,128)} %get-tuple-element.57) | copy-start | bytes 2310148
  22.1 8.2 %copy-start.10 = (f32[2,47,16,128]{3,1,2,0:T(8,128)S(1)}, f32[2,47,16,128]{3,1,2,0:T(8,128)}, u32[]{:S(2)}) copy-start(f32[2,47,16,128]{3,1,2,0:T(8,128)} %get-tuple-element.58) | copy-start | bytes 2310148
  22.1 8.2 %copy-start.13 = (f32[2,46,16,128]{3,1,2,0:T(8,128)S(1)}, f32[2,46,16,128]{3,1,2,0:T(8,128)}, u32[]{:S(2)}) copy-start(f32[2,46,16,128]{3,1,2,0:T(8,128)} %get-tuple-element.61) | copy-start | bytes 2260996
  22.1 8.2 %copy-start.14 = (f32[2,46,16,128]{3,1,2,0:T(8,128)S(1)}, f32[2,46,16,128]{3,1,2,0:T(8,128)}, u32[]{:S(2)}) copy-start(f32[2,46,16,128]{3,1,2,0:T(8,128)} %get-tuple-element.62) | copy-start | bytes 2260996
  22.1 8.2 %copy-start.17 = (f32[2,45,16,128]{3,1,2,0:T(8,128)S(1)}, f32[2,45,16,128]{3,1,2,0:T(8,128)}, u32[]{:S(2)}) copy-start(f32[2,45,16,128]{3,1,2,0:T(8,128)} %get-tuple-element.65) | copy-start | bytes 2211844
  22.2 8.2 %copy-start.18 = (f32[2,45,16,128]{3,1,2,0:T(8,128)S(1)}, f32[2,45,16,128]{3,1,2,0:T(8,128)}, u32[]{:S(2)}) copy-start(f32[2,45,16,128]{3,1,2,0:T(8,128)} %get-tuple-element.66) | copy-start | bytes 2211844
  22.2 8.2 %copy-start.19 = (f32[2,44,16,128]{3,1,2,0:T(8,128)S(1)}, f32[2,44,16,128]{3,1,2,0:T(8,128)}, u32[]{:S(2)}) copy-start(f32[2,44,16,128]{3,1,2,0:T(8,128)} %get-tuple-element.71) | copy-start | bytes 2162692
  22.2 8.2 %copy-start.20 = (f32[2,44,16,128]{3,1,2,0:T(8,128)S(1)}, f32[2,44,16,128]{3,1,2,0:T(8,128)}, u32[]{:S(2)}) copy-start(f32[2,44,16,128]{3,1,2,0:T(8,128)} %get-tuple-element.72) | copy-start | bytes 2162692
  22.2 8.2 %copy-start.35 = (f32[2,3,16,128]{3,1,2,0:T(4,128)S(1)}, f32[2,3,16,128]{3,1,2,0:T(4,128)}, u32[]{:S(2)}) copy-start(f32[2,3,16,128]{3,1,2,0:T(4,128)} %get-tuple-element.63) | copy-start | bytes 147460
  22.2 8.2 %copy-start.36 = (f32[2,3,16,128]{3,1,2,0:T(4,128)S(1)}, f32[2,3,16,128]{3,1,2,0:T(4,128)}, u32[]{:S(2)}) copy-start(f32[2,3,16,128]{3,1,2,0:T(4,128)} %get-tuple-element.64) | copy-start | bytes 147460
  22.2 8.2 %copy-start.37 = (f32[2,4,16,128]{3,1,2,0:T(4,128)S(1)}, f32[2,4,16,128]{3,1,2,0:T(4,128)}, u32[]{:S(2)}) copy-start(f32[2,4,16,128]{3,1,2,0:T(4,128)} %get-tuple-element.69) | copy-start | bytes 196612
  22.2 8.2 %copy-start.38 = (f32[2,4,16,128]{3,1,2,0:T(4,128)S(1)}, f32[2,4,16,128]{3,1,2,0:T(4,128)}, u32[]{:S(2)}) copy-start(f32[2,4,16,128]{3,1,2,0:T(4,128)} %get-tuple-element.70) | copy-start | bytes 196612
  22.2 8.2 %copy-start.43 = (f32[2,2,16,128]{3,1,2,0:T(2,128)S(1)}, f32[2,2,16,128]{3,1,2,0:T(2,128)}, u32[]{:S(2)}) copy-start(f32[2,2,16,128]{3,1,2,0:T(2,128)} %get-tuple-element.59) | copy-start | bytes 98308
  22.2 8.2 %copy-start.44 = (f32[2,2,16,128]{3,1,2,0:T(2,128)S(1)}, f32[2,2,16,128]{3,1,2,0:T(2,128)}, u32[]{:S(2)}) copy-start(f32[2,2,16,128]{3,1,2,0:T(2,128)} %get-tuple-element.60) | copy-start | bytes 98308
  45.6 4.6 %collective-permute-start.4 = (f32[2,48,16,4]{1,2,3,0:T(8,128)}, f32[2,48,16,4]{1,2,3,0:T(8,128)}, u32[]{:S(2)}, u32[]{:S(2)}) collective-permute-start(f32[2,48,16,4]{1,2,3,0:T(8,128)} %copy.119), channel_id=1, source_target_pairs={{0,8},{8,16},{16,24},{24,0},{1,9},{9,17},{17,25},{25,1},{2,10},{10... | collective-permute-start | bytes 73736 | tf_op jit(solution)/shard_map/ppermute | solution.py:20
  46.5 4.9 %collective-permute-start.5 = (f32[2,48,16,4]{1,2,3,0:T(8,128)}, f32[2,48,16,4]{1,2,3,0:T(8,128)}, u32[]{:S(2)}, u32[]{:S(2)}) collective-permute-start(f32[2,48,16,4]{1,2,3,0:T(8,128)} %copy.120), channel_id=1, source_target_pairs={{8,0},{16,8},{24,16},{0,24},{9,1},{17,9},{25,17},{1,25},{10,2},{18... | collective-permute-start | bytes 73736 | tf_op jit(solution)/shard_map/ppermute | solution.py:23
  52.6 17.7 %copy-start.2 = (f32[2,48,16,4]{3,1,2,0:T(8,128)}, f32[2,48,16,4]{3,1,2,0:T(8,128)S(1)}, u32[]{:S(2)}) copy-start(f32[2,48,16,4]{3,1,2,0:T(8,128)S(1)} %copy.122) | copy-start | bytes 73732
  52.6 17.7 %copy-start.29 = (f32[48,16,128]{2,0,1:T(8,128)S(1)}, f32[48,16,128]{2,0,1:T(8,128)}, u32[]{:S(2)}) copy-start(f32[48,16,128]{2,0,1:T(8,128)} %copy.125) | copy-start | bytes 1179652
  52.6 17.7 %copy-start.40 = (f32[2,4,16,128]{3,1,2,0:T(4,128)S(1)}, f32[2,4,16,128]{3,1,2,0:T(4,128)}, u32[]{:S(2)}) copy-start(f32[2,4,16,128]{3,1,2,0:T(4,128)} %get-tuple-element.40) | copy-start | bytes 196612
  52.7 17.7 %copy-start.41 = (f32[2,3,16,128]{3,1,2,0:T(4,128)S(1)}, f32[2,3,16,128]{3,1,2,0:T(4,128)}, u32[]{:S(2)}) copy-start(f32[2,3,16,128]{3,1,2,0:T(4,128)} %get-tuple-element.43) | copy-start | bytes 147460
  52.7 17.7 %copy-start.42 = (f32[2,3,16,128]{3,1,2,0:T(4,128)S(1)}, f32[2,3,16,128]{3,1,2,0:T(4,128)}, u32[]{:S(2)}) copy-start(f32[2,3,16,128]{3,1,2,0:T(4,128)} %get-tuple-element.44) | copy-start | bytes 147460
  52.7 17.7 %copy-start.48 = (f32[2,2,16,128]{3,1,2,0:T(2,128)S(1)}, f32[2,2,16,128]{3,1,2,0:T(2,128)}, u32[]{:S(2)}) copy-start(f32[2,2,16,128]{3,1,2,0:T(2,128)} %get-tuple-element.48) | copy-start | bytes 98308
  53.1 9.4 %collective-permute-start.6 = (f32[2,48,4,136]{3,1,2,0:T(8,128)S(1)}, f32[2,48,4,136]{3,1,2,0:T(8,128)S(1)}, u32[]{:S(2)}, u32[]{:S(2)}) collective-permute-start(f32[2,48,4,136]{3,1,2,0:T(8,128)S(1)} %get-tuple-element.13), channel_id=1, source_target_pairs={{1,0},{2,1},{3,2},{4,3},{5,4},{6,5},{7,6},{0,7},{9,8},{10,9},{11,1... | collective-permute-start | bytes 626696 | tf_op jit(solution)/shard_map/ppermute | solution.py:23
  60.3 8.8 %collective-permute-start.7 = (f32[2,48,4,136]{3,1,2,0:T(8,128)S(1)}, f32[2,48,4,136]{3,1,2,0:T(8,128)S(1)}, u32[]{:S(2)}, u32[]{:S(2)}) collective-permute-start(f32[2,48,4,136]{3,1,2,0:T(8,128)S(1)} %get-tuple-element.14), channel_id=1, source_target_pairs={{0,1},{1,2},{2,3},{3,4},{4,5},{5,6},{6,7},{7,0},{8,9},{9,10},{10,1... | collective-permute-start | bytes 626696 | tf_op jit(solution)/shard_map/ppermute | solution.py:20
  60.3 10.1 %copy-start.39 = (f32[2,4,16,128]{3,1,2,0:T(4,128)S(1)}, f32[2,4,16,128]{3,1,2,0:T(4,128)}, u32[]{:S(2)}) copy-start(f32[2,4,16,128]{3,1,2,0:T(4,128)} %get-tuple-element.39) | copy-start | bytes 196612
  60.3 10.1 %copy-start.3 = (f32[2,48,16,128]{3,1,2,0:T(8,128)S(1)}, f32[2,48,16,128]{3,1,2,0:T(8,128)}, u32[]{:S(2)}) copy-start(f32[2,48,16,128]{3,1,2,0:T(8,128)} %get-tuple-element.6) | copy-start | bytes 2359300
  60.3 10.1 %copy-start.21 = (f32[2,44,16,128]{3,1,2,0:T(8,128)S(1)}, f32[2,44,16,128]{3,1,2,0:T(8,128)}, u32[]{:S(2)}) copy-start(f32[2,44,16,128]{3,1,2,0:T(8,128)} %get-tuple-element.37) | copy-start | bytes 2162692
  60.3 10.1 %copy-start.22 = (f32[2,44,16,128]{3,1,2,0:T(8,128)S(1)}, f32[2,44,16,128]{3,1,2,0:T(8,128)}, u32[]{:S(2)}) copy-start(f32[2,44,16,128]{3,1,2,0:T(8,128)} %get-tuple-element.38) | copy-start | bytes 2162692
  60.4 10.1 %copy-start.23 = (f32[2,45,16,128]{3,1,2,0:T(8,128)S(1)}, f32[2,45,16,128]{3,1,2,0:T(8,128)}, u32[]{:S(2)}) copy-start(f32[2,45,16,128]{3,1,2,0:T(8,128)} %get-tuple-element.41) | copy-start | bytes 2211844
  60.4 10.1 %copy-start.24 = (f32[2,45,16,128]{3,1,2,0:T(8,128)S(1)}, f32[2,45,16,128]{3,1,2,0:T(8,128)}, u32[]{:S(2)}) copy-start(f32[2,45,16,128]{3,1,2,0:T(8,128)} %get-tuple-element.42) | copy-start | bytes 2211844
  60.4 10.1 %copy-start.25 = (f32[2,46,16,128]{3,1,2,0:T(8,128)S(1)}, f32[2,46,16,128]{3,1,2,0:T(8,128)}, u32[]{:S(2)}) copy-start(f32[2,46,16,128]{3,1,2,0:T(8,128)} %get-tuple-element.45) | copy-start | bytes 2260996
  60.4 10.1 %copy-start.26 = (f32[2,46,16,128]{3,1,2,0:T(8,128)S(1)}, f32[2,46,16,128]{3,1,2,0:T(8,128)}, u32[]{:S(2)}) copy-start(f32[2,46,16,128]{3,1,2,0:T(8,128)} %get-tuple-element.46) | copy-start | bytes 2260996
  60.4 10.1 %copy-start.27 = (f32[2,47,16,128]{3,1,2,0:T(8,128)S(1)}, f32[2,47,16,128]{3,1,2,0:T(8,128)}, u32[]{:S(2)}) copy-start(f32[2,47,16,128]{3,1,2,0:T(8,128)} %get-tuple-element.49) | copy-start | bytes 2310148
  60.4 10.1 %copy-start.28 = (f32[2,47,16,128]{3,1,2,0:T(8,128)S(1)}, f32[2,47,16,128]{3,1,2,0:T(8,128)}, u32[]{:S(2)}) copy-start(f32[2,47,16,128]{3,1,2,0:T(8,128)} %get-tuple-element.50) | copy-start | bytes 2310148
  60.4 10.1 %copy-start.47 = (f32[2,2,16,128]{3,1,2,0:T(2,128)S(1)}, f32[2,2,16,128]{3,1,2,0:T(2,128)}, u32[]{:S(2)}) copy-start(f32[2,2,16,128]{3,1,2,0:T(2,128)} %get-tuple-element.47) | copy-start | bytes 98308
  84.9 4.6 %collective-permute-start.8 = (f32[2,48,16,4]{1,2,3,0:T(8,128)}, f32[2,48,16,4]{1,2,3,0:T(8,128)S(1)}, u32[]{:S(2)}, u32[]{:S(2)}) collective-permute-start(f32[2,48,16,4]{1,2,3,0:T(8,128)} %copy.127), channel_id=1, source_target_pairs={{0,8},{8,16},{16,24},{24,0},{1,9},{9,17},{17,25},{25,1},{2,10},{10... | collective-permute-start | bytes 73736 | tf_op jit(solution)/shard_map/ppermute | solution.py:20
  85.4 4.4 %collective-permute-start.9 = (f32[2,48,16,4]{1,2,3,0:T(8,128)S(1)}, f32[2,48,16,4]{1,2,3,0:T(8,128)}, u32[]{:S(2)}, u32[]{:S(2)}) collective-permute-start(f32[2,48,16,4]{1,2,3,0:T(8,128)S(1)} %copy.128), channel_id=1, source_target_pairs={{8,0},{16,8},{24,16},{0,24},{9,1},{17,9},{25,17},{1,25},{10,2},{18... | collective-permute-start | bytes 73736 | tf_op jit(solution)/shard_map/ppermute | solution.py:23
  91.0 13.5 %copy-start.32 = (f32[2,3,16,128]{3,1,2,0:T(4,128)S(1)}, f32[2,3,16,128]{3,1,2,0:T(4,128)}, u32[]{:S(2)}) copy-start(f32[2,3,16,128]{3,1,2,0:T(4,128)} %get-tuple-element.28) | copy-start | bytes 147460
  91.0 13.5 %copy-start.33 = (f32[2,4,16,128]{3,1,2,0:T(4,128)S(1)}, f32[2,4,16,128]{3,1,2,0:T(4,128)}, u32[]{:S(2)}) copy-start(f32[2,4,16,128]{3,1,2,0:T(4,128)} %get-tuple-element.33) | copy-start | bytes 196612
  91.0 13.5 %copy-start.34 = (f32[2,4,16,128]{3,1,2,0:T(4,128)S(1)}, f32[2,4,16,128]{3,1,2,0:T(4,128)}, u32[]{:S(2)}) copy-start(f32[2,4,16,128]{3,1,2,0:T(4,128)} %get-tuple-element.34) | copy-start | bytes 196612
  91.0 13.5 %copy-start.46 = (f32[2,2,16,128]{3,1,2,0:T(2,128)S(1)}, f32[2,2,16,128]{3,1,2,0:T(2,128)}, u32[]{:S(2)}) copy-start(f32[2,2,16,128]{3,1,2,0:T(2,128)} %get-tuple-element.24) | copy-start | bytes 98308
  91.4 9.5 %collective-permute-start.10 = (f32[2,48,4,136]{3,1,2,0:T(8,128)S(1)}, f32[2,48,4,136]{3,1,2,0:T(8,128)S(1)}, u32[]{:S(2)}, u32[]{:S(2)}) collective-permute-start(f32[2,48,4,136]{3,1,2,0:T(8,128)S(1)} %get-tuple-element.9), channel_id=1, source_target_pairs={{1,0},{2,1},{3,2},{4,3},{5,4},{6,5},{7,6},{0,7},{9,8},{10,9},{11,1... | collective-permute-start | bytes 626696 | tf_op jit(solution)/shard_map/ppermute | solution.py:23
  95.3 7.8 %collective-permute-start.11 = (f32[2,48,4,136]{3,1,2,0:T(8,128)S(1)}, f32[2,48,4,136]{3,1,2,0:T(8,128)S(1)}, u32[]{:S(2)}, u32[]{:S(2)}) collective-permute-start(f32[2,48,4,136]{3,1,2,0:T(8,128)S(1)} %get-tuple-element.10), channel_id=1, source_target_pairs={{0,1},{1,2},{2,3},{3,4},{4,5},{5,6},{6,7},{7,0},{8,9},{9,10},{10,1... | collective-permute-start | bytes 626696 | tf_op jit(solution)/shard_map/ppermute | solution.py:20
  95.4 9.1 %copy-start.31 = (f32[2,3,16,128]{3,1,2,0:T(4,128)S(1)}, f32[2,3,16,128]{3,1,2,0:T(4,128)}, u32[]{:S(2)}) copy-start(f32[2,3,16,128]{3,1,2,0:T(4,128)} %get-tuple-element.27) | copy-start | bytes 147460
  95.4 9.1 %copy-start.4 = (f32[2,48,16,128]{3,1,2,0:T(8,128)S(1)}, f32[2,48,16,128]{3,1,2,0:T(8,128)}, u32[]{:S(2)}) copy-start(f32[2,48,16,128]{3,1,2,0:T(8,128)} %get-tuple-element.6) | copy-start | bytes 2359300
  95.4 9.1 %copy-start.5 = (f32[2,47,16,128]{3,1,2,0:T(8,128)S(1)}, f32[2,47,16,128]{3,1,2,0:T(8,128)}, u32[]{:S(2)}) copy-start(f32[2,47,16,128]{3,1,2,0:T(8,128)} %get-tuple-element.21) | copy-start | bytes 2310148
  95.4 9.1 %copy-start.6 = (f32[2,47,16,128]{3,1,2,0:T(8,128)S(1)}, f32[2,47,16,128]{3,1,2,0:T(8,128)}, u32[]{:S(2)}) copy-start(f32[2,47,16,128]{3,1,2,0:T(8,128)} %get-tuple-element.22) | copy-start | bytes 2310148
  95.4 9.1 %copy-start.7 = (f32[2,46,16,128]{3,1,2,0:T(8,128)S(1)}, f32[2,46,16,128]{3,1,2,0:T(8,128)}, u32[]{:S(2)}) copy-start(f32[2,46,16,128]{3,1,2,0:T(8,128)} %get-tuple-element.25) | copy-start | bytes 2260996
  95.5 9.1 %copy-start.8 = (f32[2,46,16,128]{3,1,2,0:T(8,128)S(1)}, f32[2,46,16,128]{3,1,2,0:T(8,128)}, u32[]{:S(2)}) copy-start(f32[2,46,16,128]{3,1,2,0:T(8,128)} %get-tuple-element.26) | copy-start | bytes 2260996
  95.5 9.1 %copy-start.11 = (f32[2,45,16,128]{3,1,2,0:T(8,128)S(1)}, f32[2,45,16,128]{3,1,2,0:T(8,128)}, u32[]{:S(2)}) copy-start(f32[2,45,16,128]{3,1,2,0:T(8,128)} %get-tuple-element.29) | copy-start | bytes 2211844
  95.5 9.1 %copy-start.12 = (f32[2,45,16,128]{3,1,2,0:T(8,128)S(1)}, f32[2,45,16,128]{3,1,2,0:T(8,128)}, u32[]{:S(2)}) copy-start(f32[2,45,16,128]{3,1,2,0:T(8,128)} %get-tuple-element.30) | copy-start | bytes 2211844
  95.5 9.1 %copy-start.15 = (f32[2,44,16,128]{3,1,2,0:T(8,128)S(1)}, f32[2,44,16,128]{3,1,2,0:T(8,128)}, u32[]{:S(2)}) copy-start(f32[2,44,16,128]{3,1,2,0:T(8,128)} %get-tuple-element.35) | copy-start | bytes 2162692
  95.5 9.1 %copy-start.16 = (f32[2,44,16,128]{3,1,2,0:T(8,128)S(1)}, f32[2,44,16,128]{3,1,2,0:T(8,128)}, u32[]{:S(2)}) copy-start(f32[2,44,16,128]{3,1,2,0:T(8,128)} %get-tuple-element.36) | copy-start | bytes 2162692
  95.5 9.1 %copy-start.45 = (f32[2,2,16,128]{3,1,2,0:T(2,128)S(1)}, f32[2,2,16,128]{3,1,2,0:T(2,128)}, u32[]{:S(2)}) copy-start(f32[2,2,16,128]{3,1,2,0:T(2,128)} %get-tuple-element.23) | copy-start | bytes 98308
where the time goes:
time: 135 us; the launch traced here: 132 us
  local copies, waits for them, and re-layouts  36.3 us (27%)
  other arithmetic  27 us (20%)
  waiting for transfers between devices  24.2 us (18%)
  starting transfers between devices  23.3 us (17%)
  blocking collectives  19.8 us (15%)
  between operations  1.55 us (1%)
    ppermute x6, starting transfers between devices, padded_2(): lax.ppermute(lax.slice_in_dim(block, 0, width, axis=dim), axis, backward)  20.9 us
    all_to_all x1, blocking collectives, sum_at_owner(): lax.all_to_all(cut_along(shard, dim, length), axis, 0, 0, tiled=True)  19.8 us
    slice x16, local copies, waits for them, and re-layouts, apply_hamiltonian(): jnp.roll(centre, offset, 1)  14.1 us
    ppermute x6, waiting for transfers between devices, padded_2(): lax.ppermute(lax.slice_in_dim(block, 0, width, axis=dim), axis, backward)  12.5 us
    ppermute x6, waiting for transfers between devices, padded_2(): lax.ppermute(lax.slice_in_dim(block, block.shape[dim] - width, None, axis...  11.7 us
    div x1, other arithmetic, apply_hamiltonian(): (-0.5 * summed + (potential_core[None] - ENERGY_SHIFT) * centre) / ENERGY...  7.65 us
    slice x8, local copies, waits for them, and re-layouts, apply_hamiltonian(): jnp.roll(centre, -offset, 1)  7.04 us
    reduce_sum x1, other arithmetic, local(): squares = jnp.sum(filtered * filtered, axis=0)  6.93 us
  transfers between devices with their start and end apart: 12, of which 8 were waited for; matrix products, arithmetic and copies ran while one was open for 11% of the time, Pallas kernels for 0%

commit v1 on v0

v1 whole, which is shorter than its diff:
```python
import jax
import jax.numpy as jnp
from jax import lax
from jax.experimental import pallas as pl
from jax.experimental.pallas import tpu as pltpu
from jax.sharding import PartitionSpec as P

MESH = pl.DeviceIdType.MESH

CHEB = 3
STENCIL = (-205.0 / 72.0, 8.0 / 5.0, -1.0 / 5.0, 8.0 / 315.0, -1.0 / 560.0)
WHOLE = (0.0, 8064.0, -1008.0, 128.0, -9.0)
SHIFT = 5.875
SPREAD = 6.0
LAP = tuple(-0.5 * s / SPREAD for s in STENCIL)
MXU_SCALE = -0.5 / SPREAD / 5040.0

NZ = 48
NORB = 2
ROWS = 16
LANES = 128
CHUNKS = 8
PLANES = NZ // CHUNKS
TILES = PLANES * NORB
TOP = 8


def split_bf16(values):
    high = values.astype(jnp.bfloat16)
    low = (values - high.astype(jnp.float32)).astype(jnp.bfloat16)
    return jnp.concatenate([high, low], axis=1)


def band_weights():
    row = lax.rem(lax.broadcasted_iota(jnp.int32, (2 * LANES, LANES), 0), LANES)
    column = lax.broadcasted_iota(jnp.int32, (2 * LANES, LANES), 1)
    distance = jnp.abs(row - column)
    weights = jnp.zeros((2 * LANES, LANES), jnp.float32)
    for j in range(1, 5):
        weights = jnp.where(distance == j, WHOLE[j], weights)
    return weights.astype(jnp.bfloat16)


def edge_weights():
    row = lax.rem(lax.broadcasted_iota(jnp.int32, (2 * LANES, LANES), 0), LANES)
    column = lax.broadcasted_iota(jnp.int32, (2 * LANES, LANES), 1)
    distance = jnp.abs(row - column)
    crosses = (row // 8 == column // 8) & (row // 4 != column // 4)
    weights = jnp.zeros((2 * LANES, LANES), jnp.float32)
    for j in range(1, 5):
        weights = jnp.where(crosses & (distance == j), WHOLE[j], weights)
    return weights.astype(jnp.bfloat16)


def kernel(
    orbitals, potential, coeffs, out,
    t0, t1, t2, acc, pot, band, edge, packed, beside, squares, arrived, forward, other,
    local_sem, y_send, y_recv, x_send, x_recv, q_send, q_recv, z_send, z_recv,
):
    terms = (t0, t1, t2)
    orb, gx, gy = lax.axis_index("orb"), lax.axis_index("gx"), lax.axis_index("gy")
    n_gx, n_gy = lax.axis_size("gx"), lax.axis_size("gy")
    ox, oz = orb // 2, lax.rem(orb, 2)

    def chunk_at(position):
        to_x = lax.rem(ox + 1 + position, 4)
        to_z = lax.rem(oz + 1 + position // 4, 2)
        return to_x * 2 + to_z

    up, down = {"gy": lax.rem(gy + 1, n_gy)}, {"gy": lax.rem(gy + n_gy - 1, n_gy)}
    right, left = {"gx": lax.rem(gx + 1, n_gx)}, {"gx": lax.rem(gx + n_gx - 1, n_gx)}

    def along_x(distance):
        return {"orb": lax.rem(ox + distance, 4) * 2 + oz}

    across = {"orb": ox * 2 + 1 - oz}

    loads = [
        pltpu.make_async_copy(
            orbitals.at[o], t0.at[:, o, pl.ds(TOP, ROWS)], local_sem.at[o]
        )
        for o in range(NORB)
    ]
    loads.append(pltpu.make_async_copy(potential, pot, local_sem.at[NORB]))
    for load in loads:
        load.start()

    barrier = pltpu.get_barrier_semaphore()
    partners = [up, down, right, left, along_x(1), along_x(2), along_x(3), across]
    for partner in partners:
        pl.semaphore_signal(barrier, inc=1, device_id=partner, device_id_type=MESH)

    def y_copy(k, planes, position, way):
        term = terms[k]
        source, target = (TOP + ROWS - 4, TOP - 4) if way == 0 else (TOP, TOP + ROWS)
        return pltpu.make_async_remote_copy(
            src_ref=term.at[planes, :, pl.ds(source, 4)],
            dst_ref=term.at[planes, :, pl.ds(target, 4)],
            send_sem=y_send.at[k, way],
            recv_sem=y_recv.at[k, position, way],
            device_id=up if way == 0 else down,
            device_id_type=MESH,
        )

    def x_copy(k, position, way):
        return pltpu.make_async_remote_copy(
            src_ref=packed.at[k, position],
            dst_ref=beside.at[k, way, position],
            send_sem=x_send.at[k, way],
            recv_sem=x_recv.at[k, position, way],
            device_id=right if way == 0 else left,
            device_id_type=MESH,
        )

    def chunk_planes(position):
        return pl.ds(chunk_at(position) * PLANES, PLANES)

    def send_edges(k, position):
        planes = chunk_planes(position)
        for way in range(2):
            y_copy(k, planes, position, way).start()
        for way in range(2):
            x_copy(k, position, way).start()

    lane = lax.broadcasted_iota(jnp.int32, (ROWS, LANES), 1)
    at_edge = (lane < 4) | (lane >= LANES - 4)

    def pack(tiles):
        result = jnp.zeros((ROWS, LANES), jnp.float32)
        for g, tile in enumerate(tiles):
            result = jnp.where(lane // 8 == g, pltpu.roll(tile, 8 * g + 4, 1), result)
        return result

    band[...] = band_weights()
    edge[...] = edge_weights()
    for load in loads:
        load.wait()

    @pl.loop(0, CHUNKS)
    def _(position):
        z = chunk_at(position) * PLANES
        packed[0, position] = pack(
            [t0[z + i, o, pl.ds(TOP, ROWS), :] for i in range(PLANES) for o in range(NORB)]
        )

    pl.semaphore_wait(barrier, len(partners))

    @pl.loop(0, CHUNKS)
    def _(position):
        send_edges(0, position)

    @pl.loop(0, NZ // 4)
    def _(i):
        rows = pl.ds(i * 4, 4)
        pot[rows] = pot[rows] * (1.0 / SPREAD) + (-SHIFT / SPREAD + 3.0 * LAP[0])

    c0, c1, c2, c3 = coeffs[0], coeffs[1], coeffs[2], coeffs[3]

    def inside(k):
        term = terms[k]

        @pl.loop(0, CHUNKS)
        def _(chunk):
            z = chunk * PLANES
            for o in range(NORB):
                planes = [
                    term[lax.rem(z + d + NZ, NZ), o, pl.ds(TOP, ROWS), :]
                    for d in range(-4, PLANES + 4)
                ]
                block = jnp.concatenate(planes[4 : 4 + PLANES], axis=0)
                along = jnp.dot(
                    split_bf16(block), band[...], preferred_element_type=jnp.float32
                )
                for i in range(PLANES):
                    centre = planes[4 + i]
                    total = pot[z + i] * centre + MXU_SCALE * along[ROWS * i : ROWS * (i + 1)]
                    for j in range(1, 5):
                        total = total + LAP[j] * (planes[4 + i - j] + planes[4 + i + j])
                    if k == 0:
                        t1[z + i, o, pl.ds(TOP, ROWS), :] = total
                    elif k == 1:
                        t2[z + i, o, pl.ds(TOP, ROWS), :] = (
                            2.0 * total - t0[z + i, o, pl.ds(TOP, ROWS), :]
                        )
                    else:
                        acc[z + i, o] = (
                            (2.0 * c3) * total
                            + c2 * centre
                            + (c1 - c3) * t1[z + i, o, pl.ds(TOP, ROWS), :]
                            + c0 * t0[z + i, o, pl.ds(TOP, ROWS), :]
                        )

    def across_edges(k, position):
        term = terms[k]
        z = chunk_at(position) * PLANES
        for way in range(2):
            x_copy(k, position, way).wait_recv()
        side = jnp.where(
            lax.rem(lane, 8) < 4, beside[k, 0, position], beside[k, 1, position]
        )
        sides = MXU_SCALE * jnp.dot(
            split_bf16(side), edge[...], preferred_element_type=jnp.float32
        )
        for way in range(2):
            y_copy(k, chunk_planes(position), position, way).wait_recv()
        totals = []
        for i in range(PLANES):
            for o in range(NORB):
                g = i * NORB + o
                total = jnp.where(at_edge, pltpu.roll(sides, LANES - 4 - 8 * g, 1), 0.0)
                for j in range(1, 5):
                    total = total + LAP[j] * (
                        term[z + i, o, pl.ds(TOP - j, ROWS), :]
                        + term[z + i, o, pl.ds(TOP + j, ROWS), :]
                    )
                totals.append(total)
        return z, totals

    for k in range(CHEB - 1):
        inside(k)
        following = terms[k + 1]

        @pl.loop(0, CHUNKS)
        def _(position):
            z, totals = across_edges(k, position)
            tiles = []
            for i in range(PLANES):
                for o in range(NORB):
                    total = totals[i * NORB + o]
                    if k > 0:
                        total = 2.0 * total
                    tile = following[z + i, o, pl.ds(TOP, ROWS), :] + total
                    following[z + i, o, pl.ds(TOP, ROWS), :] = tile
                    tiles.append(tile)
            packed[k + 1, position] = pack(tiles)
            send_edges(k + 1, position)

    def q_copy(position):
        distance = lax.rem(position, 4)
        return pltpu.make_async_remote_copy(
            src_ref=squares.at[position],
            dst_ref=arrived.at[position],
            send_sem=q_send.at[position],
            recv_sem=q_recv.at[position],
            device_id=along_x(distance + 1),
            device_id_type=MESH,
        )

    inside(CHEB - 1)

    @pl.loop(0, CHUNKS)
    def _(position):
        z, totals = across_edges(CHEB - 1, position)
        for i in range(PLANES):
            total = None
            for o in range(NORB):
                value = acc[z + i, o] + (2.0 * c3) * totals[i * NORB + o]
                total = value * value if total is None else total + value * value
            squares[position, i] = total

        @pl.when(lax.rem(position, 4) != 3)
        def _():
            q_copy(position).start()

    for position in range(3):
        q_copy(position).wait_recv()
    forward[...] = (squares[3] + arrived[0]) + (arrived[1] + arrived[2])
    to_owner = pltpu.make_async_remote_copy(
        src_ref=forward, dst_ref=other, send_sem=z_send.at[0], recv_sem=z_recv.at[0],
        device_id=across, device_id_type=MESH,
    )
    to_owner.start()

    for k in range(CHEB):
        for way in range(2):
            pltpu.make_async_remote_copy(
                src_ref=packed.at[k],
                dst_ref=beside.at[k, way],
                send_sem=x_send.at[k, way],
                recv_sem=x_recv.at[k, 0, way],
                device_id=right if way == 0 else left,
                device_id_type=MESH,
            ).wait_send()
            y_copy(k, pl.ds(0, NZ), 0, way).wait_send()
    for position in (0, 1, 2, 4, 5, 6):
        q_copy(position).wait_send()

    for position in range(4, 7):
        q_copy(position).wait_recv()
    mine = (squares[7] + arrived[4]) + (arrived[5] + arrived[6])
    to_owner.wait()
    out[...] = (mine + other[...]) * (1.0 / 16.0)


def local(orbitals, potential, coeffs):
    return pl.pallas_call(
        kernel,
        out_shape=jax.ShapeDtypeStruct((PLANES, ROWS, LANES), jnp.float32),
        in_specs=[
            pl.BlockSpec(memory_space=pl.ANY),
            pl.BlockSpec(memory_space=pl.ANY),
            pl.BlockSpec(memory_space=pltpu.SMEM),
        ],
        out_specs=pl.BlockSpec(memory_space=pltpu.VMEM),
        scratch_shapes=[
            pltpu.VMEM((NZ, NORB, 32, LANES), jnp.float32),
            pltpu.VMEM((NZ, NORB, 32, LANES), jnp.float32),
            pltpu.VMEM((NZ, NORB, 32, LANES), jnp.float32),
            pltpu.VMEM((NZ, NORB, ROWS, LANES), jnp.float32),
            pltpu.VMEM((NZ, ROWS, LANES), jnp.float32),
            pltpu.VMEM((2 * LANES, LANES), jnp.bfloat16),
            pltpu.VMEM((2 * LANES, LANES), jnp.bfloat16),
            pltpu.VMEM((CHEB, CHUNKS, ROWS, LANES), jnp.float32),
            pltpu.VMEM((CHEB, 2, CHUNKS, ROWS, LANES), jnp.float32),
            pltpu.VMEM((CHUNKS, PLANES, ROWS, LANES), jnp.float32),
            pltpu.VMEM((CHUNKS, PLANES, ROWS, LANES), jnp.float32),
            pltpu.VMEM((PLANES, ROWS, LANES), jnp.float32),
            pltpu.VMEM((PLANES, ROWS, LANES), jnp.float32),
            pltpu.SemaphoreType.DMA((NORB + 1,)),
            pltpu.SemaphoreType.DMA((CHEB, 2)),
            pltpu.SemaphoreType.DMA((CHEB, CHUNKS, 2)),
            pltpu.SemaphoreType.DMA((CHEB, 2)),
            pltpu.SemaphoreType.DMA((CHEB, CHUNKS, 2)),
            pltpu.SemaphoreType.DMA((CHUNKS,)),
            pltpu.SemaphoreType.DMA((CHUNKS,)),
            pltpu.SemaphoreType.DMA((1,)),
            pltpu.SemaphoreType.DMA((1,)),
        ],
        compiler_params=pltpu.CompilerParams(
            collective_id=0, has_side_effects=True, vmem_limit_bytes=48 * 2**20
        ),
        name="chebyshev",
    )(orbitals, potential, coeffs)


def solution(mesh):
    in_specs = (P("orb", None, "gy", "gx"), P(None, "gy", "gx"), P())
    out_specs = P("orb", "gy", "gx")
    return jax.shard_map(local, mesh=mesh, in_specs=in_specs, out_specs=out_specs, check_vma=False)
```

time: 135 us -> 36.9 us (0.27); the launches traced: 132 us -> 36.5 us
  Pallas kernels: 0 us -> 33.1 us
  local copies, waits for them, and re-layouts: 36.3 us -> 3.41 us
  other arithmetic: 27 us -> 0 us
  waiting for transfers between devices: 24.2 us -> 0 us
  starting transfers between devices: 23.3 us -> 0 us
  blocking collectives: 19.8 us -> 0 us
  between operations: 1.55 us -> 0.01 us
    pallas_call x0 -> x1, Pallas kernels: none -> 33.1 us  [local(): pl.pallas_call(kernel, out_shape=jax.ShapeDtypeStruct((PLANES, ROWS, LANE...]
    slice x32 -> x0, local copies, waits for them, and re-layouts: 27.2 us -> none  [the longest x16 14.1 us: apply_hamiltonian(): jnp.roll(centre, offset, 1)]
    ppermute x12 -> x0, waiting for transfers between devices: 24.2 us -> none  [the longest x6 12.5 us: padded_2(): lax.ppermute(lax.slice_in_dim(block, 0, width, axis=dim), axis, backward)]
    ppermute x12 -> x0, starting transfers between devices: 23.3 us -> none  [the longest x6 20.9 us: padded_2(): lax.ppermute(lax.slice_in_dim(block, 0, width, axis=dim), axis, backward)]
    all_to_all x1 -> x0, blocking collectives: 19.8 us -> none  [sum_at_owner(): lax.all_to_all(cut_along(shard, dim, length), axis, 0, 0, tiled=True)]
    div x2 -> x0, other arithmetic: 8.27 us -> none  [the longest x1 7.65 us: apply_hamiltonian(): (-0.5 * summed + (potential_core[None] - ENERGY_SHIFT) * centre) / ENERGY...]
    reduce_sum x2 -> x0, other arithmetic: 6.96 us -> none  [the longest x1 6.93 us: local(): squares = jnp.sum(filtered * filtered, axis=0)]
    sub x1 -> x0, other arithmetic: 6.71 us -> none  [local(): following = 2.0 * applied - previous]
  transfers between devices with their start and end apart: 12 -> 0, of which waited for: 8 -> 0; matrix products, arithmetic and copies ran while one was open for 11% -> 0% of each run, Pallas kernels for 0% -> 0%
where the time goes in v1:
time: 36.9 us; the launch traced here: 36.5 us
  Pallas kernels  33.1 us (90%)
  local copies, waits for them, and re-layouts  3.41 us (9%)
    pallas_call x1, Pallas kernels, local(): pl.pallas_call(kernel, out_shape=jax.ShapeDtypeStruct((PLANES, ROWS, LANE...  33.1 us
    unnamed x7, local copies, waits for them, and re-layouts  3.41 us

profile of v1, /device:TPU:1, one launch (start us, length us, event | category | flops | bytes accessed | tf_op | source)
XLA Modules:
  0.0 36.5 jit_solution(1249070578048946591)
XLA Ops:
  0.0 0.0 copy-start
  0.0 1.1 %copy-done = f32[2,48,16,128]{3,2,1,0:T(8,128)S(1)} copy-done((f32[2,48,16,128]{3,2,1,0:T(8,128)S(1)}, f32[2,48,16,128]{3,2,1,0:T(8,128)}, u32[]{:S(2)}) %copy-start) | copy-done | bytes 786456
  1.1 0.0 copy-start.1
  1.1 1.0 %copy-done.1 = f32[48,16,128]{2,1,0:T(8,128)S(1)} copy-done((f32[48,16,128]{2,1,0:T(8,128)S(1)}, f32[48,16,128]{2,1,0:T(8,128)}, u32[]{:S(2)}) %copy-start.1) | copy-done | bytes 393240
  2.1 0.0 copy-start.2
  2.1 0.7 %copy-done.2 = f32[4]{0:T(128)S(1)} copy-done((f32[4]{0:T(128)S(1)}, f32[4]{0:T(128)}, u32[]{:S(2)}) %copy-start.2) | copy-done | bytes 40
  2.8 33.1 %chebyshev.1 = f32[6,16,128]{2,1,0:T(8,128)S(1)} custom-call(f32[2,48,16,128]{3,2,1,0:T(8,128)S(1)} %copy-done, f32[48,16,128]{2,1,0:T(8,128)S(1)} %copy-done.1, f32[4]{0:T(128)S(1)} %copy-done.2), custom_call_target="tpu_custom_call" | custom-call | tf_op jit(solution)/shard_map/chebyshev/pallas_call | solution.py:296
  35.9 0.6 %copy.5 = f32[6,16,128]{2,1,0:T(8,128)} copy(f32[6,16,128]{2,1,0:T(8,128)S(1)} %chebyshev.1) | data formatting | bytes 98304
Async XLA Ops:
  0.0 1.1 %copy-start = (f32[2,48,16,128]{3,2,1,0:T(8,128)S(1)}, f32[2,48,16,128]{3,2,1,0:T(8,128)}, u32[]{:S(2)}) copy-start(f32[2,48,16,128]{3,2,1,0:T(8,128)} %orbitals.1) | copy-start | bytes 2359300
  1.1 1.0 %copy-start.1 = (f32[48,16,128]{2,1,0:T(8,128)S(1)}, f32[48,16,128]{2,1,0:T(8,128)}, u32[]{:S(2)}) copy-start(f32[48,16,128]{2,1,0:T(8,128)} %potential.1) | copy-start | bytes 1179652
  2.1 0.7 %copy-start.2 = (f32[4]{0:T(128)S(1)}, f32[4]{0:T(128)}, u32[]{:S(2)}) copy-start(f32[4]{0:T(128)} %coeffs.1) | copy-start | bytes 52

commit v2 on v1

--- a/solution.py
+++ b/solution.py
@@ -22,6 +22,9 @@
 CHUNKS = 8
 PLANES = NZ // CHUNKS
 TILES = PLANES * NORB
+SPAN = 12
+BATCH = 4
+GROUP = 2
 TOP = 8
 
 
@@ -55,7 +58,7 @@
 def kernel(
     orbitals, potential, coeffs, out,
     t0, t1, t2, acc, pot, band, edge, packed, beside, squares, arrived, forward, other,
-    local_sem, y_send, y_recv, x_send, x_recv, q_send, q_recv, z_send, z_recv,
+    small, local_sem, y_send, y_recv, x_send, x_recv, q_send, q_recv, z_send, z_recv,
 ):
     terms = (t0, t1, t2)
     orb, gx, gy = lax.axis_index("orb"), lax.axis_index("gx"), lax.axis_index("gy")
@@ -82,6 +85,7 @@
         for o in range(NORB)
     ]
     loads.append(pltpu.make_async_copy(potential, pot, local_sem.at[NORB]))
+    loads.append(pltpu.make_async_copy(coeffs, small, local_sem.at[NORB + 1]))
     for load in loads:
         load.start()
 
@@ -123,12 +127,15 @@
             x_copy(k, position, way).start()
 
     lane = lax.broadcasted_iota(jnp.int32, (ROWS, LANES), 1)
+    in_left = lax.rem(lane, 8) < 4
     at_edge = (lane < 4) | (lane >= LANES - 4)
+
+    group_of = lane // 8
 
     def pack(tiles):
         result = jnp.zeros((ROWS, LANES), jnp.float32)
         for g, tile in enumerate(tiles):
-            result = jnp.where(lane // 8 == g, pltpu.roll(tile, 8 * g + 4, 1), result)
+            result = jnp.where(group_of == g, pltpu.roll(tile, 8 * g + 4, 1), result)
         return result
 
     band[...] = band_weights()
@@ -154,55 +161,61 @@
         rows = pl.ds(i * 4, 4)
         pot[rows] = pot[rows] * (1.0 / SPREAD) + (-SHIFT / SPREAD + 3.0 * LAP[0])
 
-    c0, c1, c2, c3 = coeffs[0], coeffs[1], coeffs[2], coeffs[3]
+    c0, c1, c2, c3 = small[0], small[1], small[2], small[3]
 
     def inside(k):
         term = terms[k]
 
-        @pl.loop(0, CHUNKS)
-        def _(chunk):
-            z = chunk * PLANES
+        @pl.loop(0, NZ // SPAN)
+        def _(span):
+            z = span * SPAN
+            block = [term[z + i, o, pl.ds(TOP, ROWS), :] for o in range(NORB) for i in range(SPAN)]
+            along = MXU_SCALE * jnp.dot(
+                split_bf16(jnp.concatenate(block, axis=0)),
+                band[...],
+                preferred_element_type=jnp.float32,
+            )
             for o in range(NORB):
-                planes = [
-                    term[lax.rem(z + d + NZ, NZ), o, pl.ds(TOP, ROWS), :]
-                    for d in range(-4, PLANES + 4)
-                ]
-                block = jnp.concatenate(planes[4 : 4 + PLANES], axis=0)
-                along = jnp.dot(
-                    split_bf16(block), band[...], preferred_element_type=jnp.float32
-                )
-                for i in range(PLANES):
-                    centre = planes[4 + i]
-                    total = pot[z + i] * centre + MXU_SCALE * along[ROWS * i : ROWS * (i + 1)]
-                    for j in range(1, 5):
-                        total = total + LAP[j] * (planes[4 + i - j] + planes[4 + i + j])
-                    if k == 0:
-                        t1[z + i, o, pl.ds(TOP, ROWS), :] = total
-                    elif k == 1:
-                        t2[z + i, o, pl.ds(TOP, ROWS), :] = (
-                            2.0 * total - t0[z + i, o, pl.ds(TOP, ROWS), :]
-                        )
-                    else:
-                        acc[z + i, o] = (
-                            (2.0 * c3) * total
-                            + c2 * centre
-                            + (c1 - c3) * t1[z + i, o, pl.ds(TOP, ROWS), :]
-                            + c0 * t0[z + i, o, pl.ds(TOP, ROWS), :]
-                        )
-
-    def across_edges(k, position):
+                for half in range(0, ROWS, 8):
+                    rows = pl.ds(TOP + half, 8)
+                    planes = [
+                        term[lax.rem(z + d + NZ, NZ), o, rows, :] for d in range(-4, SPAN + 4)
+                    ]
+                    for i in range(SPAN):
+                        first = (o * SPAN + i) * ROWS + half
+                        centre = planes[4 + i]
+                        total = pot[z + i, pl.ds(half, 8)] * centre + along[first : first + 8]
+                        for j in range(1, 5):
+                            total = total + LAP[j] * (planes[4 + i - j] + planes[4 + i + j])
+                        if k == 0:
+                            t1[z + i, o, rows, :] = total
+                        elif k == 1:
+                            t2[z + i, o, rows, :] = 2.0 * total - t0[z + i, o, rows, :]
+                        else:
+                            acc[z + i, o, pl.ds(half, 8)] = (
+                                (2.0 * c3) * total
+                                + c2 * centre
+                                + (c1 - c3) * t1[z + i, o, rows, :]
+                                + c0 * t0[z + i, o, rows, :]
+                            )
+
+    def side_terms(k, base):
+        blocks = []
+        for n in range(BATCH):
+            for way in range(2):
+                x_copy(k, base + n, way).wait_recv()
+            blocks.append(
+                jnp.where(in_left, beside[k, 0, base + n], beside[k, 1, base + n])
+            )
+        return MXU_SCALE * jnp.dot(
+            split_bf16(jnp.concatenate(blocks, axis=0)),
+            edge[...],
+            preferred_element_type=jnp.float32,
+        )
+
+    def halo_terms(k, position, sides):
         term = terms[k]
         z = chunk_at(position) * PLANES
-        for way in range(2):
-            x_copy(k, position, way).wait_recv()
-        side = jnp.where(
-            lax.rem(lane, 8) < 4, beside[k, 0, position], beside[k, 1, position]
-        )
-        sides = MXU_SCALE * jnp.dot(
-            split_bf16(side), edge[...], preferred_element_type=jnp.float32
-        )
-        for way in range(2):
-            y_copy(k, chunk_planes(position), position, way).wait_recv()
         totals = []
         for i in range(PLANES):
             for o in range(NORB):
@@ -216,13 +229,26 @@
                 totals.append(total)
         return z, totals
 
+    def by_batches(k, finish, send):
+        @pl.loop(0, CHUNKS // BATCH)
+        def _(batch):
+            base = batch * BATCH
+            sides = side_terms(k, base)
+            for first in range(0, BATCH, GROUP):
+                group = range(first, first + GROUP)
+                for n in group:
+                    for way in range(2):
+                        y_copy(k, chunk_planes(base + n), base + n, way).wait_recv()
+                for n in group:
+                    finish(base + n, *halo_terms(k, base + n, sides[ROWS * n : ROWS * (n + 1)]))
+                for n in group:
+                    send(base + n, n)
+
     for k in range(CHEB - 1):
         inside(k)
-        following = terms[k + 1]
-
-        @pl.loop(0, CHUNKS)
-        def _(position):
-            z, totals = across_edges(k, position)
+
+        def finish(position, z, totals, k=k):
+            following = terms[k + 1]
             tiles = []
             for i in range(PLANES):
                 for o in range(NORB):
@@ -233,7 +259,11 @@
                     following[z + i, o, pl.ds(TOP, ROWS), :] = tile
                     tiles.append(tile)
             packed[k + 1, position] = pack(tiles)
+
+        def send(position, n, k=k):
             send_edges(k + 1, position)
+
+        by_batches(k, finish, send)
 
     def q_copy(position):
         distance = lax.rem(position, 4)
@@ -248,9 +278,7 @@
 
     inside(CHEB - 1)
 
-    @pl.loop(0, CHUNKS)
-    def _(position):
-        z, totals = across_edges(CHEB - 1, position)
+    def finish(position, z, totals):
         for i in range(PLANES):
             total = None
             for o in range(NORB):
@@ -258,9 +286,11 @@
                 total = value * value if total is None else total + value * value
             squares[position, i] = total
 
-        @pl.when(lax.rem(position, 4) != 3)
-        def _():
+    def send(position, n):
+        if n % 4 != 3:
             q_copy(position).start()
+
+    by_batches(CHEB - 1, finish, send)
 
     for position in range(3):
         q_copy(position).wait_recv()
@@ -299,7 +329,7 @@
         in_specs=[
             pl.BlockSpec(memory_space=pl.ANY),
             pl.BlockSpec(memory_space=pl.ANY),
-            pl.BlockSpec(memory_space=pltpu.SMEM),
+            pl.BlockSpec(memory_space=pl.ANY),
         ],
         out_specs=pl.BlockSpec(memory_space=pltpu.VMEM),
         scratch_shapes=[
@@ -316,7 +346,8 @@
             pltpu.VMEM((CHUNKS, PLANES, ROWS, LANES), jnp.float32),
             pltpu.VMEM((PLANES, ROWS, LANES), jnp.float32),
             pltpu.VMEM((PLANES, ROWS, LANES), jnp.float32),
-            pltpu.SemaphoreType.DMA((NORB + 1,)),
+            pltpu.SMEM((4,), jnp.float32),
+            pltpu.SemaphoreType.DMA((NORB + 2,)),
             pltpu.SemaphoreType.DMA((CHEB, 2)),
             pltpu.SemaphoreType.DMA((CHEB, CHUNKS, 2)),
             pltpu.SemaphoreType.DMA((CHEB, 2)),
@@ -327,7 +358,7 @@
             pltpu.SemaphoreType.DMA((1,)),
         ],
         compiler_params=pltpu.CompilerParams(
-            collective_id=0, has_side_effects=True, vmem_limit_bytes=48 * 2**20
+            collective_id=0, has_side_effects=True, vmem_limit_bytes=60 * 2**20
         ),
         name="chebyshev",
     )(orbitals, potential, coeffs)

time: 36.9 us -> 34.5 us (0.935)
  the two profiles are of different devices: /device:TPU:1 before, /device:TPU:32 now
where the time goes in v2:
time: 34.5 us; the launch traced here: 34.4 us
  Pallas kernels  32.9 us (95%)
  local copies, waits for them, and re-layouts  1.42 us (4%)
    pallas_call x1, Pallas kernels, local(): pl.pallas_call(kernel, out_shape=jax.ShapeDtypeStruct((PLANES, ROWS, LANE...  32.9 us
    unnamed x1, local copies, waits for them, and re-layouts  1.42 us

profile of v2, /device:TPU:32, one launch (start us, length us, event | category | flops | bytes accessed | tf_op | source)
XLA Modules:
  0.0 34.4 jit_solution(7839207983684902886)
XLA Ops:
  0.0 32.9 %chebyshev.1 = f32[6,16,128]{2,1,0:T(8,128)} custom-call(f32[2,48,16,128]{3,2,1,0:T(8,128)} %orbitals.1, f32[48,16,128]{2,1,0:T(8,128)} %potential.1, f32[4]{0:T(128)} %coeffs.1), custom_call_target="tpu_custom_call" | custom-call | tf_op jit(solution)/shard_map/chebyshev/pallas_call | solution.py:326
  32.9 1.4 %copy.5 = f32[6,16,128]{2,1,0:T(8,128)} copy(f32[6,16,128]{2,1,0:T(8,128)} %chebyshev.1) | data formatting | bytes 98304

commit v3 on v2

--- a/solution.py
+++ b/solution.py
@@ -24,7 +24,7 @@
 TILES = PLANES * NORB
 SPAN = 12
 BATCH = 4
-GROUP = 2
+GROUP = 1
 TOP = 8
 
 
@@ -65,18 +65,21 @@
     n_gx, n_gy = lax.axis_size("gx"), lax.axis_size("gy")
     ox, oz = orb // 2, lax.rem(orb, 2)
 
+    def distance_at(position):
+        return lax.rem(position + 1, 4)
+
     def chunk_at(position):
-        to_x = lax.rem(ox + 1 + position, 4)
+        to_x = lax.rem(ox + distance_at(position), 4)
         to_z = lax.rem(oz + 1 + position // 4, 2)
         return to_x * 2 + to_z
 
     up, down = {"gy": lax.rem(gy + 1, n_gy)}, {"gy": lax.rem(gy + n_gy - 1, n_gy)}
     right, left = {"gx": lax.rem(gx + 1, n_gx)}, {"gx": lax.rem(gx + n_gx - 1, n_gx)}
 
-    def along_x(distance):
-        return {"orb": lax.rem(ox + distance, 4) * 2 + oz}
-
-    across = {"orb": ox * 2 + 1 - oz}
+    core = lax.rem(gy, 2)
+
+    def at(distance, z, on_core):
+        return {"orb": lax.rem(ox + distance, 4) * 2 + z, "gy": gy - core + on_core}
 
     loads = [
         pltpu.make_async_copy(
@@ -90,7 +93,10 @@
         load.start()
 
     barrier = pltpu.get_barrier_semaphore()
-    partners = [up, down, right, left, along_x(1), along_x(2), along_x(3), across]
+    partners = [up, down, right, left]
+    for to_core in (core, 1 - core):
+        partners += [at(distance, oz, to_core) for distance in (2, 1, 3)]
+        partners.append(at(0, 1 - oz, to_core))
     for partner in partners:
         pl.semaphore_signal(barrier, inc=1, device_id=partner, device_id_type=MESH)
 
@@ -266,13 +272,30 @@
         by_batches(k, finish, send)
 
     def q_copy(position):
-        distance = lax.rem(position, 4)
+        own = position // 4
+        slot = position + 4 * (own + core * (1 - own))
         return pltpu.make_async_remote_copy(
             src_ref=squares.at[position],
-            dst_ref=arrived.at[position],
+            dst_ref=arrived.at[slot],
             send_sem=q_send.at[position],
-            recv_sem=q_recv.at[position],
-            device_id=along_x(distance + 1),
+            recv_sem=q_recv.at[slot],
+            device_id=at(distance_at(position), oz, 1 - own * (1 - core)),
+            device_id_type=MESH,
+        )
+
+    def wait_arrived(slots):
+        for slot in slots:
+            pltpu.make_async_copy(
+                squares.at[0], arrived.at[slot], q_recv.at[slot]
+            ).wait()
+
+    def to_owner(on_core):
+        return pltpu.make_async_remote_copy(
+            src_ref=forward.at[on_core],
+            dst_ref=other,
+            send_sem=z_send.at[on_core],
+            recv_sem=z_recv.at[0],
+            device_id=at(0, 1 - oz, on_core),
             device_id_type=MESH,
         )
 
@@ -289,17 +312,22 @@
     def send(position, n):
         if n % 4 != 3:
             q_copy(position).start()
+        else:
+
+            @pl.when((position == 3) & (core == 0))
+            def _():
+                q_copy(position).start()
 
     by_batches(CHEB - 1, finish, send)
 
-    for position in range(3):
-        q_copy(position).wait_recv()
-    forward[...] = (squares[3] + arrived[0]) + (arrived[1] + arrived[2])
-    to_owner = pltpu.make_async_remote_copy(
-        src_ref=forward, dst_ref=other, send_sem=z_send.at[0], recv_sem=z_recv.at[0],
-        device_id=across, device_id_type=MESH,
-    )
-    to_owner.start()
+    @pl.when(core == 1)
+    def _():
+        wait_arrived((4, 5, 6))
+        forward[1] = (squares[3] + arrived[4]) + (arrived[5] + arrived[6])
+        to_owner(1).start()
+        wait_arrived((0, 1, 2, 3))
+        forward[0] = (arrived[0] + arrived[1]) + (arrived[2] + arrived[3])
+        to_owner(0).start()
 
     for k in range(CHEB):
         for way in range(2):
@@ -315,10 +343,19 @@
     for position in (0, 1, 2, 4, 5, 6):
         q_copy(position).wait_send()
 
-    for position in range(4, 7):
-        q_copy(position).wait_recv()
-    mine = (squares[7] + arrived[4]) + (arrived[5] + arrived[6])
-    to_owner.wait()
+    @pl.when(core == 0)
+    def _():
+        q_copy(3).wait_send()
+
+    wait_arrived((8, 9, 10))
+    mine = (squares[7] + arrived[8]) + (arrived[9] + arrived[10])
+
+    @pl.when(core == 1)
+    def _():
+        for on_core in range(2):
+            to_owner(on_core).wait_send()
+
+    to_owner(0).wait_recv()
     out[...] = (mine + other[...]) * (1.0 / 16.0)
 
 
@@ -343,8 +380,8 @@
             pltpu.VMEM((CHEB, CHUNKS, ROWS, LANES), jnp.float32),
             pltpu.VMEM((CHEB, 2, CHUNKS, ROWS, LANES), jnp.float32),
             pltpu.VMEM((CHUNKS, PLANES, ROWS, LANES), jnp.float32),
-            pltpu.VMEM((CHUNKS, PLANES, ROWS, LANES), jnp.float32),
-            pltpu.VMEM((PLANES, ROWS, LANES), jnp.float32),
+            pltpu.VMEM((12, PLANES, ROWS, LANES), jnp.float32),
+            pltpu.VMEM((2, PLANES, ROWS, LANES), jnp.float32),
             pltpu.VMEM((PLANES, ROWS, LANES), jnp.float32),
             pltpu.SMEM((4,), jnp.float32),
             pltpu.SemaphoreType.DMA((NORB + 2,)),
@@ -353,12 +390,12 @@
             pltpu.SemaphoreType.DMA((CHEB, 2)),
             pltpu.SemaphoreType.DMA((CHEB, CHUNKS, 2)),
             pltpu.SemaphoreType.DMA((CHUNKS,)),
-            pltpu.SemaphoreType.DMA((CHUNKS,)),
-            pltpu.SemaphoreType.DMA((1,)),
+            pltpu.SemaphoreType.DMA((12,)),
+            pltpu.SemaphoreType.DMA((2,)),
             pltpu.SemaphoreType.DMA((1,)),
         ],
         compiler_params=pltpu.CompilerParams(
-            collective_id=0, has_side_effects=True, vmem_limit_bytes=60 * 2**20
+            collective_id=0, has_side_effects=True, vmem_limit_bytes=55000 * 2**10
         ),
         name="chebyshev",
     )(orbitals, potential, coeffs)

time: 34.5 us -> 32.4 us (0.939)
  the two profiles are of different devices: /device:TPU:32 before, /device:TPU:1 now
where the time goes in v3:
time: 32.4 us; the launch traced here: 32.3 us
  Pallas kernels  31 us (96%)
  local copies, waits for them, and re-layouts  1.28 us (4%)
    pallas_call x1, Pallas kernels, local(): pl.pallas_call(kernel, out_shape=jax.ShapeDtypeStruct((PLANES, ROWS, LANE...  31 us
    unnamed x3, local copies, waits for them, and re-layouts  1.28 us

profile of v3, /device:TPU:1, one launch (start us, length us, event | category | flops | bytes accessed | tf_op | source)
XLA Modules:
  0.0 32.3 jit_solution(1992418991814264676)
XLA Ops:
  0.0 0.0 copy-start
  0.0 0.7 %copy-done = f32[4]{0:T(128)S(1)} copy-done((f32[4]{0:T(128)S(1)}, f32[4]{0:T(128)}, u32[]{:S(2)}) %copy-start) | copy-done | bytes 40
  0.7 31.0 %chebyshev.1 = f32[6,16,128]{2,1,0:T(8,128)S(1)} custom-call(f32[2,48,16,128]{3,2,1,0:T(8,128)} %orbitals.1, f32[48,16,128]{2,1,0:T(8,128)} %potential.1, f32[4]{0:T(128)S(1)} %copy-done), custom_call_target="tpu_custom_call" | custom-call | tf_op jit(solution)/shard_map/chebyshev/pallas_call | solution.py:363
  31.7 0.6 %copy.5 = f32[6,16,128]{2,1,0:T(8,128)} copy(f32[6,16,128]{2,1,0:T(8,128)S(1)} %chebyshev.1) | data formatting | bytes 98304
Async XLA Ops:
  0.0 0.7 %copy-start = (f32[4]{0:T(128)S(1)}, f32[4]{0:T(128)}, u32[]{:S(2)}) copy-start(f32[4]{0:T(128)} %coeffs.1) | copy-start | bytes 52

commit v4 on v3

--- a/solution.py
+++ b/solution.py
@@ -58,7 +58,7 @@
 def kernel(
     orbitals, potential, coeffs, out,
     t0, t1, t2, acc, pot, band, edge, packed, beside, squares, arrived, forward, other,
-    small, local_sem, y_send, y_recv, x_send, x_recv, q_send, q_recv, z_send, z_recv,
+    small, local_sem, y_send, y_recv, x_send, x_recv, q_send, q_recv, z_send, z_recv, ready,
 ):
     terms = (t0, t1, t2)
     orb, gx, gy = lax.axis_index("orb"), lax.axis_index("gx"), lax.axis_index("gy")
@@ -66,7 +66,8 @@
     ox, oz = orb // 2, lax.rem(orb, 2)
 
     def distance_at(position):
-        return lax.rem(position + 1, 4)
+        step = lax.rem(position, 4)
+        return lax.rem(1 + 2 * step - 3 * (step // 2), 4)
 
     def chunk_at(position):
         to_x = lax.rem(ox + distance_at(position), 4)
@@ -80,6 +81,23 @@
 
     def at(distance, z, on_core):
         return {"orb": lax.rem(ox + distance, 4) * 2 + z, "gy": gy - core + on_core}
+
+    barrier = pltpu.get_barrier_semaphore()
+
+    def signal(semaphore, device):
+        pl.semaphore_signal(semaphore, inc=1, device_id=device, device_id_type=MESH)
+
+    partners = [up, down, right, left]
+    for to_core in (core, 1 - core):
+        partners += [at(distance, oz, to_core) for distance in (2, 1, 3)]
+    for partner in partners:
+        signal(barrier, partner)
+
+    @pl.when(oz == 0)
+    def _():
+        for to_core in range(2):
+            signal(barrier, at(0, 1, to_core))
+        signal(barrier, at(2, 1, core))
 
     loads = [
         pltpu.make_async_copy(
@@ -91,14 +109,6 @@
     loads.append(pltpu.make_async_copy(coeffs, small, local_sem.at[NORB + 1]))
     for load in loads:
         load.start()
-
-    barrier = pltpu.get_barrier_semaphore()
-    partners = [up, down, right, left]
-    for to_core in (core, 1 - core):
-        partners += [at(distance, oz, to_core) for distance in (2, 1, 3)]
-        partners.append(at(0, 1 - oz, to_core))
-    for partner in partners:
-        pl.semaphore_signal(barrier, inc=1, device_id=partner, device_id_type=MESH)
 
     def y_copy(k, planes, position, way):
         term = terms[k]
@@ -125,12 +135,17 @@
     def chunk_planes(position):
         return pl.ds(chunk_at(position) * PLANES, PLANES)
 
-    def send_edges(k, position):
-        planes = chunk_planes(position)
+    def y_send_start(k, position):
         for way in range(2):
-            y_copy(k, planes, position, way).start()
+            y_copy(k, chunk_planes(position), position, way).start()
+
+    def x_send_start(k, position):
         for way in range(2):
             x_copy(k, position, way).start()
+
+    def send_edges(k, position):
+        y_send_start(k, position)
+        x_send_start(k, position)
 
     lane = lax.broadcasted_iota(jnp.int32, (ROWS, LANES), 1)
     in_left = lax.rem(lane, 8) < 4
@@ -156,11 +171,15 @@
             [t0[z + i, o, pl.ds(TOP, ROWS), :] for i in range(PLANES) for o in range(NORB)]
         )
 
-    pl.semaphore_wait(barrier, len(partners))
+    pl.semaphore_wait(barrier, len(partners) + 3 * oz)
 
     @pl.loop(0, CHUNKS)
     def _(position):
         send_edges(0, position)
+
+    @pl.when(oz == 1)
+    def _():
+        signal(ready.at[0], at(0, 0, 1))
 
     @pl.loop(0, NZ // 4)
     def _(i):
@@ -264,22 +283,25 @@
                     tile = following[z + i, o, pl.ds(TOP, ROWS), :] + total
                     following[z + i, o, pl.ds(TOP, ROWS), :] = tile
                     tiles.append(tile)
+            y_send_start(k + 1, position)
             packed[k + 1, position] = pack(tiles)
 
         def send(position, n, k=k):
-            send_edges(k + 1, position)
+            x_send_start(k + 1, position)
 
         by_batches(k, finish, send)
 
     def q_copy(position):
         own = position // 4
-        slot = position + 4 * (own + core * (1 - own))
+        straight = jnp.where(position == 2, oz, 0)
+        slot = jnp.where(straight == 1, 11, position + 4 * (own + core * (1 - own)))
+        to_core = jnp.where(straight == 1, core, 1 - own * (1 - core))
         return pltpu.make_async_remote_copy(
             src_ref=squares.at[position],
             dst_ref=arrived.at[slot],
             send_sem=q_send.at[position],
             recv_sem=q_recv.at[slot],
-            device_id=at(distance_at(position), oz, 1 - own * (1 - core)),
+            device_id=at(distance_at(position), oz - straight, to_core),
             device_id_type=MESH,
         )
 
@@ -311,7 +333,11 @@
 
     def send(position, n):
         if n % 4 != 3:
-            q_copy(position).start()
+
+            @pl.when(position < 4)
+            def _():
+                q_copy(position).start()
+
         else:
 
             @pl.when((position == 3) & (core == 0))
@@ -322,12 +348,30 @@
 
     @pl.when(core == 1)
     def _():
-        wait_arrived((4, 5, 6))
-        forward[1] = (squares[3] + arrived[4]) + (arrived[5] + arrived[6])
+        wait_arrived((4, 5))
+        forward[1] = (squares[3] + arrived[4]) + arrived[5]
+
+        @pl.when(oz == 0)
+        def _():
+            pl.semaphore_wait(ready.at[0], 2)
+            wait_arrived((6,))
+            forward[1] = forward[1] + arrived[6]
+
         to_owner(1).start()
-        wait_arrived((0, 1, 2, 3))
-        forward[0] = (arrived[0] + arrived[1]) + (arrived[2] + arrived[3])
+        wait_arrived((0, 1, 3))
+        forward[0] = (arrived[0] + arrived[1]) + arrived[3]
+
+        @pl.when(oz == 0)
+        def _():
+            wait_arrived((2,))
+            forward[0] = forward[0] + arrived[2]
+
         to_owner(0).start()
+
+    for position in range(3):
+        q_copy(position).wait_send()
+    for position in range(4, 7):
+        q_copy(position).start()
 
     for k in range(CHEB):
         for way in range(2):
@@ -340,7 +384,7 @@
                 device_id_type=MESH,
             ).wait_send()
             y_copy(k, pl.ds(0, NZ), 0, way).wait_send()
-    for position in (0, 1, 2, 4, 5, 6):
+    for position in range(4, 7):
         q_copy(position).wait_send()
 
     @pl.when(core == 0)
@@ -357,6 +401,11 @@
 
     to_owner(0).wait_recv()
     out[...] = (mine + other[...]) * (1.0 / 16.0)
+
+    @pl.when(oz == 0)
+    def _():
+        wait_arrived((11,))
+        out[...] = out[...] + arrived[11] * (1.0 / 16.0)
 
 
 def local(orbitals, potential, coeffs):
@@ -393,6 +442,7 @@
             pltpu.SemaphoreType.DMA((12,)),
             pltpu.SemaphoreType.DMA((2,)),
             pltpu.SemaphoreType.DMA((1,)),
+            pltpu.SemaphoreType.REGULAR((1,)),
         ],
         compiler_params=pltpu.CompilerParams(
             collective_id=0, has_side_effects=True, vmem_limit_bytes=55000 * 2**10

time: 32.4 us -> 31.9 us (0.985)
  Pallas kernels: 31 us -> 30.5 us
    pallas_call x1, Pallas kernels: 31 us -> 30.5 us  [local(): pl.pallas_call(kernel, out_shape=jax.ShapeDtypeStruct((PLANES, ROWS, LANE...]
where the time goes in v4:
time: 31.9 us; the launch traced here: 31.8 us
  Pallas kernels  30.5 us (96%)
  local copies, waits for them, and re-layouts  1.28 us (4%)
    pallas_call x1, Pallas kernels, local(): pl.pallas_call(kernel, out_shape=jax.ShapeDtypeStruct((PLANES, ROWS, LANE...  30.5 us
    unnamed x3, local copies, waits for them, and re-layouts  1.28 us

profile of v4, /device:TPU:1, one launch (start us, length us, event | category | flops | bytes accessed | tf_op | source)
XLA Modules:
  0.0 31.8 jit_solution(15667812318904946526)
XLA Ops:
  0.0 0.0 copy-start
  0.0 0.7 %copy-done = f32[4]{0:T(128)S(1)} copy-done((f32[4]{0:T(128)S(1)}, f32[4]{0:T(128)}, u32[]{:S(2)}) %copy-start) | copy-done | bytes 40
  0.7 30.5 %chebyshev.1 = f32[6,16,128]{2,1,0:T(8,128)S(1)} custom-call(f32[2,48,16,128]{3,2,1,0:T(8,128)} %orbitals.1, f32[48,16,128]{2,1,0:T(8,128)} %potential.1, f32[4]{0:T(128)S(1)} %copy-done), custom_call_target="tpu_custom_call" | custom-call | tf_op jit(solution)/shard_map/chebyshev/pallas_call | solution.py:412
  31.2 0.6 %copy.5 = f32[6,16,128]{2,1,0:T(8,128)} copy(f32[6,16,128]{2,1,0:T(8,128)S(1)} %chebyshev.1) | data formatting | bytes 98304
Async XLA Ops:
  0.0 0.7 %copy-start = (f32[4]{0:T(128)S(1)}, f32[4]{0:T(128)}, u32[]{:S(2)}) copy-start(f32[4]{0:T(128)} %coeffs.1) | copy-start | bytes 52

commit v5 on v4

--- a/solution.py
+++ b/solution.py
@@ -23,7 +23,7 @@
 PLANES = NZ // CHUNKS
 TILES = PLANES * NORB
 SPAN = 12
-BATCH = 4
+BATCH = 2
 GROUP = 1
 TOP = 8
 
@@ -332,17 +332,9 @@
             squares[position, i] = total
 
     def send(position, n):
-        if n % 4 != 3:
-
-            @pl.when(position < 4)
-            def _():
-                q_copy(position).start()
-
-        else:
-
-            @pl.when((position == 3) & (core == 0))
-            def _():
-                q_copy(position).start()
+        @pl.when((position < 3) | ((position == 3) & (core == 0)))
+        def _():
+            q_copy(position).start()
 
     by_batches(CHEB - 1, finish, send)
 

time: 31.9 us -> 31.7 us (level)
  no operation moved by 1% of the time
where the time goes in v5:
time: 31.7 us; the launch traced here: 31.6 us
  Pallas kernels  30.3 us (96%)
  local copies, waits for them, and re-layouts  1.28 us (4%)
    pallas_call x1, Pallas kernels, local(): pl.pallas_call(kernel, out_shape=jax.ShapeDtypeStruct((PLANES, ROWS, LANE...  30.3 us
    unnamed x3, local copies, waits for them, and re-layouts  1.28 us

profile of v5, /device:TPU:1, one launch (start us, length us, event | category | flops | bytes accessed | tf_op | source)
XLA Modules:
  0.0 31.6 jit_solution(1020745071215545839)
XLA Ops:
  0.0 0.0 copy-start
  0.0 0.7 %copy-done = f32[4]{0:T(128)S(1)} copy-done((f32[4]{0:T(128)S(1)}, f32[4]{0:T(128)}, u32[]{:S(2)}) %copy-start) | copy-done | bytes 40
  0.7 30.3 %chebyshev.1 = f32[6,16,128]{2,1,0:T(8,128)S(1)} custom-call(f32[2,48,16,128]{3,2,1,0:T(8,128)} %orbitals.1, f32[48,16,128]{2,1,0:T(8,128)} %potential.1, f32[4]{0:T(128)S(1)} %copy-done), custom_call_target="tpu_custom_call" | custom-call | tf_op jit(solution)/shard_map/chebyshev/pallas_call | solution.py:404
  31.0 0.6 %copy.5 = f32[6,16,128]{2,1,0:T(8,128)} copy(f32[6,16,128]{2,1,0:T(8,128)S(1)} %chebyshev.1) | data formatting | bytes 98304
Async XLA Ops:
  0.0 0.7 %copy-start = (f32[4]{0:T(128)S(1)}, f32[4]{0:T(128)}, u32[]{:S(2)}) copy-start(f32[4]{0:T(128)} %coeffs.1) | copy-start | bytes 52

commit v6 on v5

--- a/solution.py
+++ b/solution.py
@@ -437,10 +437,10 @@
             pltpu.SemaphoreType.REGULAR((1,)),
         ],
         compiler_params=pltpu.CompilerParams(
-            collective_id=0, has_side_effects=True, vmem_limit_bytes=55000 * 2**10
+            collective_id=0, has_side_effects=True, vmem_limit_bytes=48000 * 2**10
         ),
         name="chebyshev",
-    )(orbitals, potential, coeffs)
+    )(*(pltpu.with_memory_space_constraint(a, pltpu.HBM) for a in (orbitals, potential, coeffs)))
 
 
 def solution(mesh):

time: 31.7 us -> 31.1 us (0.981)
  local copies, waits for them, and re-layouts: 1.28 us -> 0.62 us
    unnamed x3 -> x1, local copies, waits for them, and re-layouts: 1.28 us -> 0.62 us
where the time goes in v6:
time: 31.1 us; the launch traced here: 31 us
  Pallas kernels  30.3 us (97%)
  local copies, waits for them, and re-layouts  0.62 us (2%)
    pallas_call x1, Pallas kernels, local(): pl.pallas_call(kernel, out_shape=jax.ShapeDtypeStruct((PLANES, ROWS, LANE...  30.3 us
    unnamed x1, local copies, waits for them, and re-layouts  0.62 us

profile of v6, /device:TPU:1, one launch (start us, length us, event | category | flops | bytes accessed | tf_op | source)
XLA Modules:
  0.0 31.0 jit_solution(723836521915951626)
XLA Ops:
  0.0 30.3 %chebyshev.1 = f32[6,16,128]{2,1,0:T(8,128)S(1)} custom-call(f32[2,48,16,128]{3,2,1,0:T(8,128)} %orbitals.1, f32[48,16,128]{2,1,0:T(8,128)} %potential.1, f32[4]{0:T(128)} %coeffs.1), custom_call_target="tpu_custom_call" | custom-call | tf_op jit(solution)/shard_map/chebyshev/pallas_call | solution.py:404
  30.3 0.6 %copy.5 = f32[6,16,128]{2,1,0:T(8,128)} copy(f32[6,16,128]{2,1,0:T(8,128)S(1)} %chebyshev.1) | data formatting | bytes 98304

commit v7 on v6

--- a/solution.py
+++ b/solution.py
@@ -392,16 +392,16 @@
             to_owner(on_core).wait_send()
 
     to_owner(0).wait_recv()
-    out[...] = (mine + other[...]) * (1.0 / 16.0)
+    out[...] = mine + other[...]
 
     @pl.when(oz == 0)
     def _():
         wait_arrived((11,))
-        out[...] = out[...] + arrived[11] * (1.0 / 16.0)
+        out[...] = out[...] + arrived[11]
 
 
 def local(orbitals, potential, coeffs):
-    return pl.pallas_call(
+    squares = pl.pallas_call(
         kernel,
         out_shape=jax.ShapeDtypeStruct((PLANES, ROWS, LANES), jnp.float32),
         in_specs=[
@@ -441,6 +441,7 @@
         ),
         name="chebyshev",
     )(*(pltpu.with_memory_space_constraint(a, pltpu.HBM) for a in (orbitals, potential, coeffs)))
+    return squares * (1.0 / 16.0)
 
 
 def solution(mesh):

time: 31.1 us -> 31.1 us (level)
  other arithmetic: 0 us -> 0.63 us
  local copies, waits for them, and re-layouts: 0.62 us -> 0 us
    mul x0 -> x1, other arithmetic: none -> 0.63 us  [local(): return squares * (1.0 / 16.0)]
    unnamed x1 -> x0, local copies, waits for them, and re-layouts: 0.62 us -> none
where the time goes in v7:
time: 31.1 us; the launch traced here: 31 us
  Pallas kernels  30.3 us (97%)
  other arithmetic  0.63 us (2%)
    pallas_call x1, Pallas kernels, local(): pl.pallas_call(kernel, out_shape=jax.ShapeDtypeStruct((PLANES, ROWS, LANE...  30.3 us
    mul x1, other arithmetic, local(): return squares * (1.0 / 16.0)  0.63 us

profile of v7, /device:TPU:1, one launch (start us, length us, event | category | flops | bytes accessed | tf_op | source)
XLA Modules:
  0.0 31.0 jit_solution(2230269924467628020)
XLA Ops:
  0.0 30.3 %chebyshev.1 = f32[6,16,128]{2,1,0:T(8,128)S(1)} custom-call(f32[2,48,16,128]{3,2,1,0:T(8,128)} %orbitals.1, f32[48,16,128]{2,1,0:T(8,128)} %potential.1, f32[4]{0:T(128)} %coeffs.1), custom_call_target="tpu_custom_call" | custom-call | tf_op jit(solution)/shard_map/chebyshev/pallas_call | solution.py:404
  30.3 0.6 %broadcast_multiply_fusion = f32[6,16,128]{2,1,0:T(8,128)} fusion(f32[6,16,128]{2,1,0:T(8,128)S(1)} %chebyshev.1), kind=kLoop, calls=%fused_computation | loop fusion | flops 12288 | bytes 98304 | tf_op jit(solution)/shard_map/mul | solution.py:444
